TPU v7x, 256 devices: a whole 4x4x8 slice. The times are simulated.
256 devices in a mesh: band: 4 (over z_hi), slab: 64 (over y, x, z_lo, core).
Axes of the slice: x: 4, y: 4, z: 8 (z_hi: 4, z_lo: 2; z = z_hi * 2 + z_lo), core: 2. Of those that a mesh axis runs over, the one named last changes fastest.
Arguments:
- orbitals: float32 [2, 64, 128, 128, 128], P(None, 'band', 'slab'), may hold values from -6 to 6
- occupations: float32 [64], P('band'), may hold values from 0.01 to 0.1
- rest_density: float32 [128, 128, 128], P('slab'), may hold values from 1 to 8
- ionic_potential: float32 [128, 128, 128], P('slab'), may hold values from -6 to 6
Outputs:
- taylor_term: float32 [2, 64, 128, 128, 128], P(None, 'band', 'slab')
- potential: float32 [128, 128, 128], P('slab')
All inputs are finite; a program needn't handle non-finite values.
Results may differ from a plain program's by a relative error of at most 0.0003.
Values sent between devices are 32-bit elements; how exact they have to be, the bound alone decides.
A program may use at most 64 MiB of HBM per device.

v0:
```python
import math

import jax
import jax.numpy as jnp
from jax import lax
from jax.sharding import PartitionSpec as P

grid_spacing = 0.4
time_step = 0.01
exchange_factor = (3.0 / math.pi) ** (1.0 / 3.0)


def wavenumbers(indices, points):
    signed = jnp.where(indices < points // 2, indices, indices - points)
    return 2.0 * math.pi / (points * grid_spacing) * signed.astype(jnp.float32)


def dft_matrix(points, inverse):
    indices = jnp.arange(points, dtype=jnp.int32)
    products = indices[:, None] * indices[None, :] % points
    angles = 2.0 * math.pi / points * products.astype(jnp.float32)
    cosine = jnp.cos(angles)
    sine = jnp.sin(angles)
    if inverse:
        cosine = cosine / points
        sine = sine / points
        return jnp.stack([jnp.stack([cosine, sine]), jnp.stack([-sine, cosine])])
    return jnp.stack([jnp.stack([cosine, -sine]), jnp.stack([sine, cosine])])


def transform(values_in, matrix, dimension):
    letter_set = "abcdefg"[: values_in.ndim - 1]
    source = "p" + letter_set[: dimension - 1] + "n" + letter_set[dimension:]
    target = "q" + letter_set[: dimension - 1] + "k" + letter_set[dimension:]
    return jnp.einsum(
        source + ",pqnk->" + target, values_in, matrix, precision=lax.Precision.HIGHEST
    )


def local(orbitals, occupations, rest_density, ionic_potential):
    points = orbitals.shape[3]
    pencil_rows = points // lax.axis_size("slab")
    forward = dft_matrix(points, False)
    backward = dft_matrix(points, True)
    axis_waves = wavenumbers(jnp.arange(points, dtype=jnp.int32), points)
    local_waves = wavenumbers(
        lax.axis_index("slab") * pencil_rows + jnp.arange(pencil_rows, dtype=jnp.int32), points
    )
    pencil_g2 = (
        (axis_waves * axis_waves)[:, None, None]
        + (local_waves * local_waves)[None, :, None]
        + (axis_waves * axis_waves)[None, None, :]
    )
    kinetic = 0.5 * pencil_g2
    positive = pencil_g2 > 0
    green = jnp.where(positive, 4.0 * math.pi / jnp.where(positive, pencil_g2, 1.0), 0.0)
    squares = orbitals[0] * orbitals[0] + orbitals[1] * orbitals[1]
    partial_sum = jnp.einsum("o,oxyz->xyz", occupations, squares, precision=lax.Precision.HIGHEST)
    density = rest_density + lax.psum(partial_sum, "band")
    exchange_xc = -exchange_factor * jnp.cbrt(density)
    density_field = jnp.stack([density, jnp.zeros_like(density)])
    density_spectrum = transform(transform(density_field, forward, 3), forward, 2)
    orbital_spectrum = transform(transform(orbitals, forward, 4), forward, 3)

    def line_work(pencil, factor):
        dimension = pencil.ndim - 3
        spectrum = transform(pencil, forward, dimension) * factor
        return transform(spectrum, backward, dimension)

    density_moved = lax.all_to_all(
        density_spectrum, "slab", split_axis=2, concat_axis=1, tiled=True
    )
    density_back = lax.all_to_all(
        line_work(density_moved, green), "slab", split_axis=1, concat_axis=2, tiled=True
    )
    orbital_back = lax.all_to_all(
        line_work(
            lax.all_to_all(orbital_spectrum, "slab", split_axis=3, concat_axis=2, tiled=True),
            kinetic,
        ),
        "slab",
        split_axis=2,
        concat_axis=3,
        tiled=True,
    )
    hartree = transform(transform(density_back, backward, 2), backward, 3)[0]
    potential = ionic_potential + hartree + exchange_xc
    kinetic_part = transform(transform(orbital_back, backward, 3), backward, 4)
    applied_real = kinetic_part[0] + potential * orbitals[0]
    applied_imag = kinetic_part[1] + potential * orbitals[1]
    taylor_term = jnp.stack([time_step * applied_imag, -time_step * applied_real])
    return (taylor_term, potential)


def solution(mesh):
    return jax.shard_map(
        local,
        mesh=mesh,
        in_specs=(
            P(None, "band", "slab", None, None),
            P("band"),
            P("slab", None, None),
            P("slab", None, None),
        ),
        out_specs=(P(None, "band", "slab", None, None), P("slab", None, None)),
        check_vma=False,
    )
```

profile of v0, /device:TPU:45, one launch (start us, length us, event | category | flops | bytes accessed | tf_op | source)
XLA Modules:
  0.0 291.2 jit_solution(13866735366369932686)
XLA Ops:
  7.2 4.7 %fusion.75 = (f32[1,16,2,128,128]{4,3,2,1,0:T(8,128)}, f32[1,16,2,128,128]{4,3,2,1,0:T(8,128)}) fusion(f32[2,16,2,128,128]{4,3,2,1,0:T(8,128)} %param.4), kind=kLoop, calls=%fused_computation.99 | loop fusion | bytes 8388608 | tf_op jit(solution)/shard_map/slice | solution.py:57
  13.9 2.9 %copy.140 = f32[1,16,2,128,128]{3,4,2,1,0:T(8,128)} copy(f32[1,16,2,128,128]{4,3,2,1,0:T(8,128)} %get-tuple-element.13) | data formatting | bytes 4194304
  16.8 3.5 %add_bitcast_fusion = f32[16,2,128,128]{2,3,1,0:T(8,128)} fusion(f32[1,16,2,128,128]{3,4,2,1,0:T(8,128)S(1)} %copy.141, f32[1,16,2,128,128]{3,4,2,1,0:T(8,128)} %copy.140), kind=kLoop, calls=%fused_computation.22 | loop fusion | flops 1572864 | bytes 6291456 | tf_op jit(solution)/shard_map/add | solution.py:57
  20.3 3.1 %copy.101 = f32[16,2,128,128]{3,0,2,1:T(8,128)} copy(f32[16,2,128,128]{2,3,1,0:T(8,128)} %add_bitcast_fusion) | data formatting | bytes 4194304 | tf_op jit(solution)/shard_map/add | solution.py:57
  23.3 3.4 %fusion.63 = f32[1,2,128,128]{3,0,2,1:T(1,128)} fusion(f32[16,2,128,128]{3,0,2,1:T(8,128)} %copy.101, f32[16]{0:T(128)S(1)} %copy-done), kind=kOutput, calls=%fused_computation.86 | convolution fusion | flops 6291456 | bytes 2228288 | tf_op jit(solution)/shard_map/o,oxyz->xyz/dot_general | solution.py:58
  27.4 49.1 %all-reduce.3.cloned.1.call-done = f32[2,128,128]{2,1,0:T(8,128)} async-done(((f32[2,128,128]{2,1,0:T(8,128)}), f32[2,128,128]{2,1,0:T(8,128)}) %all-reduce.3.cloned.1.call-update) | async-done | bytes 131088 | tf_op jit(solution)/shard_map/psum | solution.py:59
  79.2 11.5 %all-to-all-start.2 = ((f32[2,2,128,128]{3,1,0,2:T(2,128)}), f32[2,2,128,128]{3,1,0,2:T(2,128)S(1)}, u32[]{:S(2)}, u32[]{:S(2)}) async-start(f32[2,2,128,128]{3,1,0,2:T(2,128)} %copy.74), calls=%async_computation.2 | async-start | bytes 524288 | tf_op jit(solution)/shard_map/all_to_all | solution.py:70
  90.7 5.5 %fusion.11 = f32[2,128,16,2,128,1]{4,1,5,0,3,2:T(8,128)S(1)} fusion(f32[1,2,128,128]{2,3,0,1:T(8,128)S(1)} %get-tuple-element.20, f32[1,2,128,128]{2,3,0,1:T(8,128)S(1)} %get-tuple-element.19, f32[2,16,2,128,128]{4,3,2,1,0:T(8,128)} %param.4), kind=kOutput, calls=%fused_computation.13 | convolution fusion | flops 3221291008 | bytes 8650752 | tf_op jit(solution)/shard_map/pabcn,pqnk->qabck/dot_general | solution.py:35
  96.2 3.8 %fusion.13 = f32[2,16,2,128,128]{4,3,2,1,0:T(8,128)S(1)} fusion(f32[2,128,16,2,128,1]{4,1,5,0,3,2:T(8,128)S(1)} %fusion.11, f32[1,2,128,128]{2,3,0,1:T(8,128)S(1)} %get-tuple-element.20, f32[1,2,128,128]{2,3,0,1:T(8,128)S(1)} %get-tuple-element.19), kind=kOutput, calls=%fused_computation.15 | convolution fusion | flops 3221291008 | bytes 8650752 | tf_op jit(solution)/shard_map/pabnd,pqnk->qabkd/dot_general | solution.py:35
  100.0 5.2 %copy.60 = f32[2,16,2,128,128]{4,2,1,0,3:T(2,128)} copy(f32[2,16,2,128,128]{4,3,2,1,0:T(8,128)S(1)} %fusion.13) | data formatting | bytes 8388608 | tf_op jit(solution)/shard_map/pabnd,pqnk->qabkd/transpose | solution.py:35
  106.0 9.0 %all-to-all-start = ((f32[2,16,2,128,128]{4,2,1,0,3:T(2,128)}), f32[2,16,2,128,128]{4,2,1,0,3:T(2,128)}, u32[]{:S(2)}, u32[]{:S(2)}) async-start(f32[2,16,2,128,128]{4,2,1,0,3:T(2,128)} %copy.60), calls=%async_computation | async-start | bytes 8388608 | tf_op jit(solution)/shard_map/all_to_all | solution.py:78
  118.6 52.2 %all-to-all-done = f32[2,16,2,128,128]{4,2,1,0,3:T(2,128)} async-done(((f32[2,16,2,128,128]{4,2,1,0,3:T(2,128)}), f32[2,16,2,128,128]{4,2,1,0,3:T(2,128)}, u32[]{:S(2)}, u32[]{:S(2)}) %all-to-all-start) | async-done | bytes 4194336 | tf_op jit(solution)/shard_map/all_to_all | solution.py:78
  170.8 8.1 %all-to-all-start.3 = ((f32[2,128,2,128]{3,2,0,1:T(2,128)}), f32[2,128,2,128]{3,2,0,1:T(2,128)}, u32[]{:S(2)}, u32[]{:S(2)}) async-start(f32[2,128,2,128]{3,2,0,1:T(2,128)} %copy.78), calls=%async_computation.3 | async-start | bytes 524288 | tf_op jit(solution)/shard_map/all_to_all | solution.py:73
  179.0 2.6 copy.61
  182.2 6.2 %fusion.9 = f32[2,128,16,2,128,1]{4,1,5,0,3,2:T(8,128)S(1)} fusion(f32[2,16,128,2,128,1]{4,1,3,2,0,5:T(8,128)S(1)} %bitcast.187, f32[1,2,128,128]{2,3,0,1:T(8,128)S(1)} %get-tuple-element.20, f32[1,2,128,128]{2,3,0,1:T(8,128)S(1)} %get-tuple-element.19), kind=kOutput, calls=%fused_computation.11 | convolution fusion | flops 3221291008 | bytes 8650752 | tf_op jit(solution)/shard_map/pancd,pqnk->qakcd/dot_general | solution.py:35
  188.4 3.7 %fusion.19 = f32[2,16,128,2,128]{4,2,3,1,0:T(8,128)S(1)} fusion(f32[2,128,16,2,128,1]{4,1,5,0,3,2:T(8,128)S(1)} %fusion.9, f32[128,2,128]{2,0,1:T(8,128)S(1)} %get-tuple-element.22, f32[2,2,128,128,1,1]{2,3,1,0,5,4:T(8,128)S(1)} %get-tuple-element.16), kind=kOutput, calls=%fused_computation.17 | convolution fusion | flops 3222274048 | bytes 8781824 | tf_op jit(solution)/shard_map/pancd,pqnk->qakcd/dot_general | solution.py:35
  192.2 5.5 %copy.65 = f32[2,16,128,2,128]{4,3,1,0,2:T(2,128)} copy(f32[2,16,128,2,128]{4,2,3,1,0:T(8,128)S(1)} %fusion.19) | data formatting | bytes 8388608 | tf_op jit(solution)/shard_map/pancd,pqnk->qakcd/transpose | solution.py:35
  197.6 9.2 %all-to-all-start.1 = ((f32[2,16,128,2,128]{4,3,1,0,2:T(2,128)}), f32[2,16,128,2,128]{4,3,1,0,2:T(2,128)}, u32[]{:S(2)}, u32[]{:S(2)}) async-start(f32[2,16,128,2,128]{4,3,1,0,2:T(2,128)} %copy.65), calls=%async_computation.1 | async-start | bytes 8388608 | tf_op jit(solution)/shard_map/all_to_all | solution.py:76
  208.9 53.7 %all-to-all-done.1 = f32[2,16,128,2,128]{4,3,1,0,2:T(2,128)} async-done(((f32[2,16,128,2,128]{4,3,1,0,2:T(2,128)}), f32[2,16,128,2,128]{4,3,1,0,2:T(2,128)}, u32[]{:S(2)}, u32[]{:S(2)}) %all-to-all-start.1) | async-done | bytes 4194336 | tf_op jit(solution)/shard_map/all_to_all | solution.py:76
  262.6 2.7 copy.66
  265.9 5.1 %fusion.2 = f32[2,128,16,2,128,1]{4,1,0,5,3,2:T(8,128)S(1)} fusion(f32[2,16,2,128,128,1]{4,1,3,2,0,5:T(8,128)S(1)} %bitcast.186, f32[1,2,128,128]{2,3,1,0:T(8,128)S(1)} %get-tuple-element.18, f32[1,2,128,128]{2,3,1,0:T(8,128)S(1)} %get-tuple-element.17), kind=kOutput, calls=%fused_computation.3 | convolution fusion | flops 3221291008 | bytes 8650752 | tf_op jit(solution)/shard_map/pabnd,pqnk->qabkd/dot_general | solution.py:35
  271.0 4.1 %fusion.16 = f32[2,16,2,128,128]{3,4,2,1,0:T(8,128)S(1)} fusion(f32[2,128,16,2,128,1]{4,1,0,5,3,2:T(8,128)S(1)} %fusion.2, f32[2,2,128,128,1,1]{2,3,1,0,5,4:T(8,128)S(1)} %get-tuple-element.16), kind=kOutput, calls=%fused_computation.16 | convolution fusion | flops 3221225472 | bytes 8650752 | tf_op jit(solution)/shard_map/pabcn,pqnk->qabck/dot_general | solution.py:35
  276.3 2.4 pad_maximum_fusion
  278.8 5.3 %copy.85 = f32[2,16,2,128,128]{4,3,2,1,0:T(8,128)} copy(f32[2,16,2,128,128]{3,4,2,1,0:T(8,128)} %pad_maximum_fusion) | data formatting | bytes 8388608
  (50 shorter events, 13.9 us)
Async XLA Ops:
  7.2 16.2 %copy-start = (f32[16]{0:T(128)S(1)}, f32[16]{0:T(128)}, u32[]{:S(2)}) copy-start(f32[16]{0:T(128)} %param.5) | copy-start | bytes 196
  7.2 69.3 %all-reduce.3.cloned.1.call-start = ((), (), s32[]{:S(2)}) async-start(), calls=%async_computation.4 | async-start | bytes 262144 | tf_op jit(solution)/shard_map/psum | solution.py:59
  20.3 56.2 %copy-start.4 = (f32[2,128,128]{2,1,0:T(8,128)S(1)}, f32[2,128,128]{2,1,0:T(8,128)}, u32[]{:S(2)}) copy-start(f32[2,128,128]{2,1,0:T(8,128)} %param.6) | copy-start | bytes 393220
  79.2 26.1 %all-to-all-start.2 = ((f32[2,2,128,128]{3,1,0,2:T(2,128)}), f32[2,2,128,128]{3,1,0,2:T(2,128)S(1)}, u32[]{:S(2)}, u32[]{:S(2)}) async-start(f32[2,2,128,128]{3,1,0,2:T(2,128)} %copy.74), calls=%async_computation.2 | async-start | bytes 524288 | tf_op jit(solution)/shard_map/all_to_all | solution.py:70
  105.3 0.7 copy-start.3
  106.0 64.8 %all-to-all-start = ((f32[2,16,2,128,128]{4,2,1,0,3:T(2,128)}), f32[2,16,2,128,128]{4,2,1,0,3:T(2,128)}, u32[]{:S(2)}, u32[]{:S(2)}) async-start(f32[2,16,2,128,128]{4,2,1,0,3:T(2,128)} %copy.60), calls=%async_computation | async-start | bytes 8388608 | tf_op jit(solution)/shard_map/all_to_all | solution.py:78
  170.8 26.8 %all-to-all-start.3 = ((f32[2,128,2,128]{3,2,0,1:T(2,128)}), f32[2,128,2,128]{3,2,0,1:T(2,128)}, u32[]{:S(2)}, u32[]{:S(2)}) async-start(f32[2,128,2,128]{3,2,0,1:T(2,128)} %copy.78), calls=%async_computation.3 | async-start | bytes 524288 | tf_op jit(solution)/shard_map/all_to_all | solution.py:73
  197.6 11.0 %copy-start.5 = (f32[2,128,128]{2,1,0:T(8,128)S(1)}, f32[2,128,128]{2,1,0:T(8,128)}, u32[]{:S(2)}) copy-start(f32[2,128,128]{2,1,0:T(8,128)} %param.6) | copy-start | bytes 393220
  197.6 11.0 %copy-start.6 = (f32[2,128,128]{2,1,0:T(8,128)S(1)}, f32[2,128,128]{2,1,0:T(8,128)}, u32[]{:S(2)}) copy-start(f32[2,128,128]{2,1,0:T(8,128)} %all-reduce.3.cloned.1.call-done) | copy-start | bytes 393220
  197.6 11.1 %copy-start.8 = (f32[2,128,128]{2,1,0:T(8,128)S(1)}, f32[2,128,128]{2,1,0:T(8,128)}, u32[]{:S(2)}) copy-start(f32[2,128,128]{2,1,0:T(8,128)} %param.7) | copy-start | bytes 393220
  197.6 65.0 %all-to-all-start.1 = ((f32[2,16,128,2,128]{4,3,1,0,2:T(2,128)}), f32[2,16,128,2,128]{4,3,1,0,2:T(2,128)}, u32[]{:S(2)}, u32[]{:S(2)}) async-start(f32[2,16,128,2,128]{4,3,1,0,2:T(2,128)} %copy.65), calls=%async_computation.1 | async-start | bytes 8388608 | tf_op jit(solution)/shard_map/all_to_all | solution.py:76
  208.8 56.5 %copy-start.7 = (f32[2,128,128]{2,1,0:T(8,128)}, f32[2,128,128]{2,1,0:T(8,128)S(1)}, u32[]{:S(2)}) copy-start(f32[2,128,128]{2,1,0:T(8,128)S(1)} %fusion.46) | copy-start | bytes 393220
  271.0 4.2 %copy-start.2 = (f32[1,16,2,128,128]{3,4,2,1,0:T(8,128)S(1)}, f32[1,16,2,128,128]{3,4,2,1,0:T(8,128)}, u32[]{:S(2)}) copy-start(f32[1,16,2,128,128]{3,4,2,1,0:T(8,128)} %copy.140) | copy-start | bytes 6291460
  276.3 7.8 %copy-start.1 = (f32[16]{0:T(128)S(1)}, f32[16]{0:T(128)}, u32[]{:S(2)}) copy-start(f32[16]{0:T(128)} %param.5) | copy-start | bytes 196
Sparse Core Ops, SparseCore 0:
  26.9 49.5 all-reduce.2
where the time goes:
time: 296 us; the launch traced here: 291 us
  waiting for transfers between devices  155 us (52%)
  local copies, waits for them, and re-layouts  40 us (14%)
  starting transfers between devices  37.9 us (13%)
  matrix products  34.4 us (12%)
  between operations  14.6 us (5%)
  other arithmetic  9.46 us (3%)
    all_to_all x1, waiting for transfers between devices, local(): lax.all_to_all(line_work(lax.all_to_all(orbital_spectrum, 'slab', split_a...  53.7 us
    all_to_all x1, waiting for transfers between devices, local(): lax.all_to_all(orbital_spectrum, 'slab', split_axis=3, concat_axis=2, til...  52.2 us
    psum x1, waiting for transfers between devices, local(): density = rest_density + lax.psum(partial_sum, 'band')  49.1 us
    dot_general x12, matrix products, transform(): jnp.einsum(source + ',pqnk->' + target, values_in, matrix, precision=lax....  30.9 us
    transpose x3, local copies, waits for them, and re-layouts, transform(): jnp.einsum(source + ',pqnk->' + target, values_in, matrix, precision=lax....  11.6 us
    all_to_all x1, starting transfers between devices, local(): lax.all_to_all(density_spectrum, 'slab', split_axis=2, concat_axis=1, til...  11.5 us
    unnamed x21, local copies, waits for them, and re-layouts  10.9 us
    all_to_all x1, starting transfers between devices, local(): lax.all_to_all(line_work(lax.all_to_all(orbital_spectrum, 'slab', split_a...  9.16 us
  transfers between devices with their start and end apart: 5, of which 3 were waited for; matrix products, arithmetic and copies ran while one was open for 14% of the time, Pallas kernels for 0%

commit v1 on v0

v1 whole, which is shorter than its diff:
```python
import math

import jax
import jax.numpy as jnp
import numpy as np
from jax import lax
from jax.sharding import PartitionSpec as P

grid_spacing = 0.4
time_step = 0.01
exchange_factor = (3.0 / math.pi) ** (1.0 / 3.0)


def wavenumbers_squared(points):
    indices = np.arange(points)
    signed = np.where(indices < points // 2, indices, indices - points)
    return (2.0 * math.pi / (points * grid_spacing) * signed) ** 2


def real_basis(points):
    j = np.arange(points)[:, None]
    x = np.arange(points)[None, :]
    cosine = np.cos(2.0 * math.pi * (j * x % points) / points)
    sine = np.sin(2.0 * math.pi * ((points - j) * x % points) / points)
    rows = np.where(j <= points // 2, cosine, sine) * math.sqrt(2.0 / points)
    return np.where((j == 0) | (j == points // 2), rows * math.sqrt(0.5), rows)


def local(orbitals, occupations, rest_density, ionic_potential):
    points = orbitals.shape[3]
    pencil_rows = points // lax.axis_size("slab")
    basis64 = real_basis(points)
    squared64 = wavenumbers_squared(points)
    basis = jnp.asarray(basis64, jnp.float32)
    kinetic = jnp.asarray(basis64.T @ (0.5 * squared64[:, None] * basis64), jnp.float32)
    squared = jnp.asarray(squared64, jnp.float32)

    def product(spec, a, b):
        return jnp.einsum(spec, a, b, precision=lax.Precision.HIGHEST)

    pencil = lax.all_to_all(orbitals, "slab", split_axis=3, concat_axis=2, tiled=True)
    first_back = lax.all_to_all(
        product("poxyz,xk->pokyz", pencil, kinetic), "slab", split_axis=2, concat_axis=3, tiled=True
    )

    squares = orbitals[0] * orbitals[0] + orbitals[1] * orbitals[1]
    partial_sum = jnp.sum(occupations[:, None, None, None] * squares, axis=0)
    density = rest_density + lax.psum(partial_sum, "band")
    exchange_xc = -exchange_factor * jnp.cbrt(density)
    spectrum = product("xkz,jk->xjz", product("xyz,kz->xyk", density, basis), basis)
    spectrum = lax.all_to_all(spectrum, "slab", split_axis=1, concat_axis=0, tiled=True)
    own_squared = lax.dynamic_slice(squared, (lax.axis_index("slab") * pencil_rows,), (pencil_rows,))
    g2 = squared[:, None, None] + own_squared[None, :, None] + squared[None, None, :]
    positive = g2 > 0
    green = jnp.where(positive, 4.0 * math.pi / jnp.where(positive, g2, 1.0), 0.0)
    lines = product("xyz,kx->kyz", spectrum, basis) * green
    lines = product("kyz,kx->xyz", lines, basis)
    back = lax.all_to_all(lines, "slab", split_axis=0, concat_axis=1, tiled=True)
    hartree = product("xkz,ky->xyz", product("xyk,kz->xyz", back, basis), basis)
    potential = ionic_potential + hartree + exchange_xc

    planes = product("poxyz,yk->poxkz", orbitals, kinetic) + product("poxyz,zk->poxyk", orbitals, kinetic)
    applied = first_back + planes + potential * orbitals
    taylor_term = jnp.stack([time_step * applied[1], -time_step * applied[0]])
    return (taylor_term, potential)


def solution(mesh):
    return jax.shard_map(
        local,
        mesh=mesh,
        in_specs=(
            P(None, "band", "slab", None, None),
            P("band"),
            P("slab", None, None),
            P("slab", None, None),
        ),
        out_specs=(P(None, "band", "slab", None, None), P("slab", None, None)),
        check_vma=False,
    )
```

time: 296 us -> 252 us (0.85)
  the two profiles are of different devices: /device:TPU:45 before, /device:TPU:1 now
where the time goes in v1:
time: 252 us; the launch traced here: 250 us
  waiting for transfers between devices  150 us (60%)
  starting transfers between devices  36.7 us (15%)
  local copies, waits for them, and re-layouts  21.9 us (9%)
  matrix products  21.4 us (8%)
  between operations  14.3 us (6%)
  other arithmetic  5.54 us (2%)
    all_to_all x1, waiting for transfers between devices, local(): lax.all_to_all(orbitals, 'slab', split_axis=3, concat_axis=2, tiled=True)  52 us
    psum x1, waiting for transfers between devices, local(): density = rest_density + lax.psum(partial_sum, 'band')  51.7 us
    all_to_all x1, waiting for transfers between devices, local(): lax.all_to_all(product('poxyz,xk->pokyz', pencil, kinetic), 'slab', split...  44.8 us
    dot_general x9, matrix products, product(): return jnp.einsum(spec, a, b, precision=lax.Precision.HIGHEST)  21.4 us
    all_to_all x1, starting transfers between devices, local(): lax.all_to_all(spectrum, 'slab', split_axis=1, concat_axis=0, tiled=True)  10.2 us
    all_to_all x1, starting transfers between devices, local(): lax.all_to_all(lines, 'slab', split_axis=0, concat_axis=1, tiled=True)  10 us
    all_to_all x1, starting transfers between devices, local(): lax.all_to_all(product('poxyz,xk->pokyz', pencil, kinetic), 'slab', split...  9.17 us
    all_to_all x1, starting transfers between devices, local(): lax.all_to_all(orbitals, 'slab', split_axis=3, concat_axis=2, tiled=True)  7.28 us
  transfers between devices with their start and end apart: 5, of which 4 were waited for; matrix products, arithmetic and copies ran while one was open for 12% of the time, Pallas kernels for 0%

profile of v1, /device:TPU:1, one launch (start us, length us, event | category | flops | bytes accessed | tf_op | source)
XLA Modules:
  0.0 250.3 jit_solution(11452314291655349051)
XLA Ops:
  7.2 2.8 %fusion.7 = f32[2,128,128]{2,1,0:T(8,128)S(1)} fusion(f32[2,16,2,128,128]{4,3,2,1,0:T(8,128)} %param.7, f32[16]{0:T(128)} %param.8), kind=kLoop, calls=%fused_computation.10 | loop fusion | flops 2588672 | bytes 4325440 | tf_op jit(solution)/shard_map/reduce_sum | solution.py:47
  10.0 0.8 copy.33
  10.9 51.7 %all-reduce.2.cloned.1.call-done = f32[2,128,128]{1,2,0:T(8,128)} async-done(((f32[2,128,128]{1,2,0:T(8,128)}), f32[2,128,128]{1,2,0:T(8,128)}) %all-reduce.2.cloned.1.call-update) | async-done | bytes 131088 | tf_op jit(solution)/shard_map/psum | solution.py:48
  62.6 1.2 fusion.13
  64.1 0.8 copy.37
  64.9 10.2 %all-to-all-start.2 = ((f32[2,128,128]{2,0,1:T(2,128)}), f32[2,128,128]{2,0,1:T(2,128)S(1)}, u32[]{:S(2)}, u32[]{:S(2)}) async-start(f32[2,128,128]{2,0,1:T(2,128)} %copy.37), calls=%async_computation.2 | async-start | bytes 262144 | tf_op jit(solution)/shard_map/all_to_all | solution.py:51
  75.1 6.6 %copy.27 = f32[2,16,2,128,128]{4,1,2,0,3:T(8,128)} copy(f32[2,16,2,128,128]{4,3,2,1,0:T(8,128)} %param.7) | data formatting | bytes 8388608 | tf_op args[0]
  81.7 1.9 all-to-all-done.2
  83.6 7.3 %all-to-all-start = ((f32[2,16,2,128,128]{4,1,2,0,3:T(8,128)}), f32[2,16,2,128,128]{4,1,2,0,3:T(8,128)}, u32[]{:S(2)}, u32[]{:S(2)}) async-start(f32[2,16,2,128,128]{4,1,2,0,3:T(8,128)} %copy.27), calls=%async_computation | async-start | bytes 8388608 | tf_op jit(solution)/shard_map/all_to_all | solution.py:41
  91.4 0.3 fusion.16
  91.7 0.8 copy.41
  92.4 52.0 %all-to-all-done = f32[2,16,2,128,128]{4,1,2,0,3:T(8,128)} async-done(((f32[2,16,2,128,128]{4,1,2,0,3:T(8,128)}), f32[2,16,2,128,128]{4,1,2,0,3:T(8,128)}, u32[]{:S(2)}, u32[]{:S(2)}) %all-to-all-start) | async-done | bytes 4194336 | tf_op jit(solution)/shard_map/all_to_all | solution.py:41
  144.5 10.0 %all-to-all-start.3 = ((f32[128,2,128]{2,1,0:T(2,128)}), f32[128,2,128]{2,1,0:T(2,128)S(1)}, u32[]{:S(2)}, u32[]{:S(2)}) async-start(f32[128,2,128]{2,1,0:T(2,128)} %copy.41), calls=%async_computation.3 | async-start | bytes 262144 | tf_op jit(solution)/shard_map/all_to_all | solution.py:58
  154.5 2.6 %copy.28 = f32[2,16,2,128,128]{4,1,3,2,0:T(8,128)S(1)} copy(f32[2,16,2,128,128]{4,1,2,0,3:T(8,128)} %all-to-all-done) | data formatting | bytes 8388608 | tf_op jit(solution)/shard_map/all_to_all | solution.py:41
  157.1 6.1 %fusion.4 = f32[2,16,128,2,128]{4,2,3,1,0:T(8,128)S(1)} fusion(f32[128,128,1,1,1]{0,1,4,3,2:T(8,128)S(1)} %copy-done.8, f32[2,16,128,2,128]{4,1,3,2,0:T(8,128)S(1)} %bitcast.56), kind=kOutput, calls=%fused_computation.6 | convolution fusion | flops 1610612736 | bytes 8454144 | tf_op jit(solution)/shard_map/poxyz,xk->pokyz/dot_general | solution.py:39
  163.2 5.2 %copy.30 = f32[2,16,128,2,128]{4,3,1,0,2:T(2,128)} copy(f32[2,16,128,2,128]{4,2,3,1,0:T(8,128)S(1)} %fusion.4) | data formatting | bytes 8388608 | tf_op jit(solution)/shard_map/poxyz,xk->pokyz/transpose | solution.py:39
  168.5 9.2 %all-to-all-start.1 = ((f32[2,16,128,2,128]{4,3,1,0,2:T(2,128)}), f32[2,16,128,2,128]{4,3,1,0,2:T(2,128)}, u32[]{:S(2)}, u32[]{:S(2)}) async-start(f32[2,16,128,2,128]{4,3,1,0,2:T(2,128)} %copy.30), calls=%async_computation.1 | async-start | bytes 8388608 | tf_op jit(solution)/shard_map/all_to_all | solution.py:42
  177.8 7.9 %fusion.15 = f32[128,2,16,2,128]{4,0,3,2,1:T(8,128)} fusion(f32[128,128,1,1,1]{0,1,4,3,2:T(8,128)S(1)} %copy-done.5, f32[2,16,2,128,128]{4,3,2,1,0:T(8,128)} %param.7), kind=kOutput, calls=%fused_computation.24 | convolution fusion | flops 1610612736 | bytes 8454144 | tf_op jit(solution)/shard_map/poxyz,yk->poxkz/dot_general | solution.py:39
  185.7 0.3 fusion.17
  186.5 44.8 %all-to-all-done.1 = f32[2,16,128,2,128]{4,3,1,0,2:T(2,128)} async-done(((f32[2,16,128,2,128]{4,3,1,0,2:T(2,128)}), f32[2,16,128,2,128]{4,3,1,0,2:T(2,128)}, u32[]{:S(2)}, u32[]{:S(2)}) %all-to-all-start.1) | async-done | bytes 4194336 | tf_op jit(solution)/shard_map/all_to_all | solution.py:42
  231.2 4.7 %copy.31 = f32[2,16,64,2,2,128]{5,4,2,3,1,0:T(2,128)S(1)} copy(f32[2,16,64,2,2,128]{5,4,1,0,3,2:T(2,128)} %bitcast.4) | data formatting | bytes 8388608 | tf_op jit(solution)/shard_map/all_to_all | solution.py:42
  236.0 4.8 %fusion.1 = f32[2,16,2,128,128]{4,3,2,1,0:T(8,128)S(1)} fusion(f32[2,16,2,128,128]{4,3,2,1,0:T(8,128)S(1)} %bitcast.57, f32[128,2,16,2,128]{4,0,3,2,1:T(8,128)S(1)} %copy-done.1, f32[2,16,2,128,128]{4,3,2,1,0:T(8,128)S(1)} %copy-done, f32[128,128,1,1,1]{0,1,4,3,2:T(8,128)S(1)} %copy-done.5, f32[2,128,128]{2,1,0:T(8,128)S(1)} %copy.45), kind=kOutput, calls=%fused_computation.3 | convolution fusion | flops 1614807040 | bytes 16973824 | tf_op jit(solution)/shard_map/poxyz,zk->poxyk/dot_general | solution.py:39
  240.7 0.4 slice_multiply_fusion.1
  241.2 2.3 pad_maximum_fusion
  (35 shorter events, 1.4 us)
Async XLA Ops:
  7.2 55.5 %copy-start.2 = (f32[128,128,1]{1,0,2:T(8,128)S(1)}, f32[128,128,1]{1,0,2:T(8,128)}, u32[]{:S(2)}) copy-start(f32[128,128,1]{1,0,2:T(8,128)} %constant.43) | copy-start | bytes 196612
  7.2 3.6 %copy-start.6 = (f32[2,128,128]{2,1,0:T(8,128)S(1)}, f32[2,128,128]{2,1,0:T(8,128)}, u32[]{:S(2)}) copy-start(f32[2,128,128]{2,1,0:T(8,128)} %param.9) | copy-start | bytes 393220
  7.2 55.5 %all-reduce.2.cloned.1.call-start = ((), (), s32[]{:S(2)}) async-start(), calls=%async_computation.4 | async-start | bytes 262144 | tf_op jit(solution)/shard_map/psum | solution.py:48
  64.9 18.7 %all-to-all-start.2 = ((f32[2,128,128]{2,0,1:T(2,128)}), f32[2,128,128]{2,0,1:T(2,128)S(1)}, u32[]{:S(2)}, u32[]{:S(2)}) async-start(f32[2,128,128]{2,0,1:T(2,128)} %copy.37), calls=%async_computation.2 | async-start | bytes 262144 | tf_op jit(solution)/shard_map/all_to_all | solution.py:51
  81.7 9.2 %copy-start.9 = (f32[128]{0:T(128)S(1)}, f32[128]{0:T(128)}, u32[]{:S(2)}) copy-start(f32[128]{0:T(128)} %constant.31.clone) | copy-start | bytes 1540
  81.7 9.4 %copy-start.10 = (f32[128,128,1]{1,0,2:T(8,128)S(1)}, f32[128,128,1]{1,0,2:T(8,128)}, u32[]{:S(2)}) copy-start(f32[128,128,1]{1,0,2:T(8,128)} %constant.44) | copy-start | bytes 196612
  83.6 60.9 %all-to-all-start = ((f32[2,16,2,128,128]{4,1,2,0,3:T(8,128)}), f32[2,16,2,128,128]{4,1,2,0,3:T(8,128)}, u32[]{:S(2)}, u32[]{:S(2)}) async-start(f32[2,16,2,128,128]{4,1,2,0,3:T(8,128)} %copy.27), calls=%async_computation | async-start | bytes 8388608 | tf_op jit(solution)/shard_map/all_to_all | solution.py:41
  144.5 24.0 %all-to-all-start.3 = ((f32[128,2,128]{2,1,0:T(2,128)}), f32[128,2,128]{2,1,0:T(2,128)S(1)}, u32[]{:S(2)}, u32[]{:S(2)}) async-start(f32[128,2,128]{2,1,0:T(2,128)} %copy.41), calls=%async_computation.3 | async-start | bytes 262144 | tf_op jit(solution)/shard_map/all_to_all | solution.py:58
  154.5 2.6 %copy-start.8 = (f32[128,128,1,1,1]{0,1,4,3,2:T(8,128)S(1)}, f32[128,128,1,1,1]{0,1,4,3,2:T(8,128)}, u32[]{:S(2)}) copy-start(f32[128,128,1,1,1]{0,1,4,3,2:T(8,128)} %constant.41) | copy-start | bytes 196612
  168.5 9.2 %copy-start.7 = (f32[2,128,128]{2,1,0:T(8,128)S(1)}, f32[2,128,128]{2,1,0:T(8,128)}, u32[]{:S(2)}) copy-start(f32[2,128,128]{2,1,0:T(8,128)} %param.10) | copy-start | bytes 393220
  168.5 9.3 %copy-start.5 = (f32[128,128,1,1,1]{0,1,4,3,2:T(8,128)S(1)}, f32[128,128,1,1,1]{0,1,4,3,2:T(8,128)}, u32[]{:S(2)}) copy-start(f32[128,128,1,1,1]{0,1,4,3,2:T(8,128)} %constant.42) | copy-start | bytes 196612
  168.5 62.7 %all-to-all-start.1 = ((f32[2,16,128,2,128]{4,3,1,0,2:T(2,128)}), f32[2,16,128,2,128]{4,3,1,0,2:T(2,128)}, u32[]{:S(2)}, u32[]{:S(2)}) async-start(f32[2,16,128,2,128]{4,3,1,0,2:T(2,128)} %copy.30), calls=%async_computation.1 | async-start | bytes 8388608 | tf_op jit(solution)/shard_map/all_to_all | solution.py:42
  177.8 8.3 %copy-start.4 = (f32[2,128,128]{1,2,0:T(8,128)S(1)}, f32[2,128,128]{1,2,0:T(8,128)}, u32[]{:S(2)}) copy-start(f32[2,128,128]{1,2,0:T(8,128)} %all-reduce.2.cloned.1.call-done) | copy-start | bytes 393220
  186.5 49.5 %copy-start.3 = (f32[2,128,128]{2,1,0:T(8,128)}, f32[2,128,128]{2,1,0:T(8,128)S(1)}, u32[]{:S(2)}) copy-start(f32[2,128,128]{2,1,0:T(8,128)S(1)} %copy.45) | copy-start | bytes 393220
  231.2 4.7 %copy-start = (f32[2,16,2,128,128]{4,3,2,1,0:T(8,128)S(1)}, f32[2,16,2,128,128]{4,3,2,1,0:T(8,128)}, u32[]{:S(2)}) copy-start(f32[2,16,2,128,128]{4,3,2,1,0:T(8,128)} %param.7) | copy-start | bytes 12582916
  231.2 4.7 %copy-start.1 = (f32[128,2,16,2,128]{4,0,3,2,1:T(8,128)S(1)}, f32[128,2,16,2,128]{4,0,3,2,1:T(8,128)}, u32[]{:S(2)}) copy-start(f32[128,2,16,2,128]{4,0,3,2,1:T(8,128)} %fusion.15) | copy-start | bytes 12582916
Sparse Core Ops, SparseCore 0:
  11.2 51.3 all-reduce.1

commit v2 on v1

v2 whole, which is shorter than its diff:
```python
import functools
import math

import jax
import jax.numpy as jnp
import numpy as np
from jax import lax
from jax.experimental import pallas as pl
from jax.experimental.pallas import tpu as pltpu
from jax.sharding import PartitionSpec as P

MESH = pl.DeviceIdType.MESH
grid_spacing = 0.4
time_step = 0.01
exchange_factor = (3.0 / math.pi) ** (1.0 / 3.0)
CHUNKS = 4


def wavenumbers_squared(points):
    indices = np.arange(points)
    signed = np.where(indices < points // 2, indices, indices - points)
    return (2.0 * math.pi / (points * grid_spacing) * signed) ** 2


def real_basis(points):
    j = np.arange(points)[:, None]
    x = np.arange(points)[None, :]
    cosine = np.cos(2.0 * math.pi * (j * x % points) / points)
    sine = np.sin(2.0 * math.pi * ((points - j) * x % points) / points)
    rows = np.where(j <= points // 2, cosine, sine) * math.sqrt(2.0 / points)
    return np.where((j == 0) | (j == points // 2), rows * math.sqrt(0.5), rows)


def kinetic_matrix(points):
    basis = real_basis(points)
    return basis.T @ (0.5 * wavenumbers_squared(points)[:, None] * basis)


def split(values):
    high = values.astype(jnp.bfloat16)
    return high, (values - high.astype(jnp.float32)).astype(jnp.bfloat16)


def dot(a, b):
    return jnp.dot(a, b, preferred_element_type=jnp.float32)


def left(matrix_high, matrix_low, values):
    high, low = split(values)
    return dot(jnp.concatenate([matrix_high, matrix_high], 1), jnp.concatenate([high, low], 0)) + dot(matrix_low, high)


def right(values, matrix_high, matrix_low):
    high, low = split(values)
    return dot(jnp.concatenate([high, low], 1), jnp.concatenate([matrix_high, matrix_high], 0)) + dot(high, matrix_low)


def exact(a, b):
    return jnp.dot(a, b, precision=lax.Precision.HIGHEST, preferred_element_type=jnp.float32)


def partner(me, step):
    step = lax.rem(step * 37, 64)
    y = lax.rem(me // 16 + step // 16, 4)
    x = lax.rem(lax.rem(me // 4, 4) + lax.rem(step // 4, 4), 4)
    return y * 16 + x * 4 + jnp.bitwise_xor(lax.rem(me, 4), lax.rem(step, 4))


def remote(source, target, send, recv, device):
    pltpu.make_async_remote_copy(
        src_ref=source, dst_ref=target, send_sem=send, recv_sem=recv, device_id=device, device_id_type=MESH
    ).start()


def wait_bytes(part, sem):
    pltpu.make_async_copy(part, part, sem).wait()


def kernel(
    high_ref, low_ref, basis_ref, basis_t_ref, occupations_ref, psi_hbm, rest_hbm, ionic_hbm, out_hbm, potential_ref,
    psi, pen, res, back, acc, rest, ionic, part, shares, density, spectrum, lines_in, lines_out, spectrum_back,
    load_sem, small_sem, out_sem, fwd_send, fwd_recv, bwd_send, bwd_recv, small_send, small_recv,
):
    band, me = lax.axis_index("band"), lax.axis_index("slab")
    points = psi.shape[-1]
    load = pltpu.make_async_copy(psi_hbm, psi, load_sem)
    load.start()
    load_rest = pltpu.make_async_copy(rest_hbm, rest, small_sem.at[0])
    load_rest.start()
    load_ionic = pltpu.make_async_copy(ionic_hbm, ionic, small_sem.at[1])
    load_ionic.start()
    barrier = pltpu.get_barrier_semaphore()

    @pl.loop(1, 64)
    def _(step):
        pl.semaphore_signal(barrier, inc=1, device_id=(band, partner(me, step)), device_id_type=MESH)

    for step in range(1, 4):
        pl.semaphore_signal(barrier, inc=1, device_id=(lax.rem(band + step, 4), me), device_id_type=MESH)

    load.wait()
    pl.semaphore_wait(barrier, 66)

    def field_part(ref, owner, c):
        rows = pl.ds(pl.multiple_of(owner // 4 * 8, 8), 8)
        return ref.at[:, lax.rem(owner, 4) * 4 + c, :, rows, :]

    def forward(c):
        @pl.loop(1, 64)
        def _(step):
            other = partner(me, step)
            remote(field_part(psi, other, c), pen.at[c, :, me], fwd_send.at[c], fwd_recv.at[c], (band, other))

        pltpu.make_async_copy(field_part(psi, me, c), pen.at[c, :, me], fwd_recv.at[c]).start()

    def backward(c):
        @pl.loop(1, 64)
        def _(step):
            other = partner(me, step)
            remote(res.at[c, :, other], field_part(back, me, c), bwd_send.at[c], bwd_recv.at[c], (band, other))

        pltpu.make_async_copy(res.at[c, :, me], field_part(back, me, c), bwd_recv.at[c]).start()

    def lines(c):
        wait_bytes(pen.at[c], fwd_recv.at[c])
        source, target = pen.reshape(CHUNKS, 2, 8 * points, points), res.reshape(CHUNKS, 2, 8 * points, points)
        for row in range(8):
            rows = pl.ds(row, points, stride=8)
            values = jnp.concatenate([source[c, 0, rows, :], source[c, 1, rows, :]], 1)
            values = left(high_ref[...], low_ref[...], values)
            target[c, 0, rows, :] = values[:, :points]
            target[c, 1, rows, :] = values[:, points:]

    def planes(c):
        @pl.loop(0, 8)
        def _(i):
            o, x = i // 2 * 4 + c, lax.rem(i, 2)
            real, imag = psi[0, o, x], psi[1, o, x]
            along_y = left(high_ref[...], low_ref[...], jnp.concatenate([real, imag], 1))
            along_z = right(jnp.concatenate([real, imag], 0), high_ref[...], low_ref[...])
            acc[0, o, x] = along_y[:, :points] + along_z[:points]
            acc[1, o, x] = along_y[:, points:] + along_z[points:]

    def finish(c):
        wait_bytes(pen.at[c], bwd_recv.at[c])

        @pl.loop(0, 8)
        def _(i):
            o, x = i // 2 * 4 + c, lax.rem(i, 2)
            potential = potential_ref[x]
            real = acc[0, o, x] + back[0, o, x] + potential * psi[0, o, x]
            imag = acc[1, o, x] + back[1, o, x] + potential * psi[1, o, x]
            acc[0, o, x] = imag
            acc[1, o, x] = -real
            pltpu.make_async_copy(acc.at[:, o, x], out_hbm.at[:, o, x], out_sem).start()

    def quarter(ref, owner):
        return ref.at[:, pl.ds(pl.multiple_of(owner * 32, 32), 32), :]

    def density_share():
        @pl.loop(0, 8)
        def _(i):
            x, rows = i // 4, pl.ds(pl.multiple_of(lax.rem(i, 4) * 32, 32), 32)
            total = jnp.zeros((32, points), jnp.float32)
            for o in range(16):
                real, imag = psi[0, o, x, rows, :], psi[1, o, x, rows, :]
                total = total + occupations_ref[o] * (real * real + imag * imag)
            part[x, rows, :] = total

        for step in range(1, 4):
            other = lax.rem(band + step, 4)
            remote(quarter(part, other), shares.at[step - 1], small_send.at[0], small_recv.at[0], (other, me))

    def density_sum():
        wait_bytes(shares, small_recv.at[0])
        load_rest.wait()
        rows = pl.ds(pl.multiple_of(band * 32, 32), 32)
        density[:, rows, :] = rest[:, rows, :] + (part[:, rows, :] + shares[0] + shares[1] + shares[2])
        for step in range(1, 4):
            other = lax.rem(band + step, 4)
            remote(quarter(density, band), quarter(density, band), small_send.at[1], small_recv.at[1], (other, me))

    def owner_of(block):
        return block * 4 + lax.rem(block, 4)

    block = me // 4
    owns = owner_of(block) == me

    def block_of(ref, i):
        return ref.at[:, pl.ds(pl.multiple_of(i * 8, 8), 8), :]

    def spectrum_send():
        wait_bytes(shares, small_recv.at[1])
        half = exact(density[...].reshape(2 * points, points), basis_t_ref[...])
        both = exact(basis_ref[...], jnp.concatenate([half[:points], half[points:]], 1))
        spectrum[0] = both[:, :points]
        spectrum[1] = both[:, points:]

        @pl.loop(0, 16)
        def _(i):
            i = lax.rem(i + block, 16)
            owner = owner_of(i)

            @pl.when(owner != me)
            def _():
                remote(block_of(spectrum, i), lines_in.at[me], small_send.at[2], small_recv.at[2], (band, owner))

            @pl.when(owner == me)
            def _():
                pltpu.make_async_copy(block_of(spectrum, i), lines_in.at[me], small_recv.at[2]).start()

    def hartree_lines():
        @pl.when(owns)
        def _():
            wait_bytes(lines_in, small_recv.at[2])
            source, target = lines_in.reshape(8 * points, points), lines_out.reshape(8 * points, points)

            def folded(i):
                return jnp.minimum(i, points - i)

            kx = folded(lax.broadcasted_iota(jnp.int32, (points, points), 0))
            kz = folded(lax.broadcasted_iota(jnp.int32, (points, points), 1))
            unit = 4.0 * math.pi * (points * grid_spacing / (2.0 * math.pi)) ** 2

            def green(row):
                ky = folded(block * 8 + row)
                square = kx * kx + kz * kz + ky * ky
                return jnp.where(square > 0, unit / jnp.maximum(square, 1).astype(jnp.float32), 0.0)

            for row in range(0, 8, 2):
                first, second = pl.ds(row, points, stride=8), pl.ds(row + 1, points, stride=8)
                values = exact(basis_ref[...], jnp.concatenate([source[first, :], source[second, :]], 1))
                values = values * jnp.concatenate([green(row), green(row + 1)], 1)
                values = exact(basis_t_ref[...], values)
                target[first, :] = values[:, :points]
                target[second, :] = values[:, points:]

            @pl.loop(1, 64)
            def _(step):
                other = partner(me, step)
                remote(lines_out.at[other], block_of(spectrum_back, block), small_send.at[3], small_recv.at[3], (band, other))

            pltpu.make_async_copy(lines_out.at[me], block_of(spectrum_back, block), small_recv.at[3]).start()

    def potential_sum():
        wait_bytes(spectrum_back, small_recv.at[3])
        half = exact(spectrum_back[...].reshape(2 * points, points), basis_ref[...])
        both = exact(basis_t_ref[...], jnp.concatenate([half[:points], half[points:]], 1))
        load_ionic.wait()
        for x in range(2):
            here = density[x]
            root = jnp.exp(jnp.log(here) * (1.0 / 3.0))
            root = root - (root * root * root - here) / (3.0 * root * root)
            potential_ref[x] = ionic[x] + both[:, x * points : (x + 1) * points] - exchange_factor * root

    forward(0)
    density_share()
    forward(1)
    planes(0)
    density_sum()
    forward(2)
    planes(1)
    spectrum_send()
    forward(3)
    lines(0)
    backward(0)
    hartree_lines()
    planes(2)
    lines(1)
    backward(1)
    planes(3)
    potential_sum()
    lines(2)
    backward(2)
    lines(3)
    backward(3)
    for c in range(CHUNKS):
        finish(c)

    for c in range(CHUNKS):
        wait_bytes(pen.at[c, :, pl.ds(0, 63)], fwd_send.at[c])
        wait_bytes(pen.at[c, :, pl.ds(0, 63)], bwd_send.at[c])
    wait_bytes(shares, small_send.at[0])
    wait_bytes(shares, small_send.at[1])

    @pl.when(owns)
    def _():
        wait_bytes(lines_in.at[pl.ds(0, 15)], small_send.at[2])
        wait_bytes(lines_in.at[pl.ds(0, 63)], small_send.at[3])

    @pl.when(jnp.logical_not(owns))
    def _():
        wait_bytes(lines_in.at[pl.ds(0, 16)], small_send.at[2])

    pltpu.make_async_copy(acc, out_hbm, out_sem).wait()


def local(orbitals, occupations, rest_density, ionic_potential):
    points = orbitals.shape[3]
    high, low = split(jnp.asarray(kinetic_matrix(points), jnp.float32))
    basis = real_basis(points)
    slab_shape = rest_density.shape
    field, slab = pltpu.VMEM(orbitals.shape, jnp.float32), pltpu.VMEM(slab_shape, jnp.float32)
    pencil = pltpu.VMEM((CHUNKS, 2, 64, 2, 8, points), jnp.float32)
    lines = pltpu.VMEM((64, 2, 8, points), jnp.float32)
    dma = pltpu.SemaphoreType.DMA
    in_vmem, anywhere = pl.BlockSpec(memory_space=pltpu.VMEM), pl.BlockSpec(memory_space=pl.ANY)
    applied, potential = pl.pallas_call(
        kernel,
        out_shape=(
            jax.ShapeDtypeStruct(orbitals.shape, jnp.float32),
            jax.ShapeDtypeStruct(slab_shape, jnp.float32),
        ),
        in_specs=[in_vmem] * 4 + [pl.BlockSpec(memory_space=pltpu.SMEM)] + [anywhere] * 3,
        out_specs=(anywhere, in_vmem),
        scratch_shapes=[
            field, pencil, pencil, field, field, slab, slab, slab,
            pltpu.VMEM((3, 2, 32, points), jnp.float32), slab, slab, lines, lines, slab,
            dma, dma((2,)), dma, dma((CHUNKS,)), dma((CHUNKS,)), dma((CHUNKS,)), dma((CHUNKS,)), dma((4,)), dma((4,)),
        ],
        compiler_params=pltpu.CompilerParams(collective_id=0, has_side_effects=True, vmem_limit_bytes=40 * 2**20),
        cost_estimate=pl.CostEstimate(flops=10**10, bytes_accessed=2**25, transcendentals=0),
    )(
        high, low, jnp.asarray(basis, jnp.float32), jnp.asarray(basis.T, jnp.float32),
        occupations, orbitals, rest_density, ionic_potential,
    )
    return (time_step * applied, potential)


def solution(mesh):
    return jax.shard_map(
        local,
        mesh=mesh,
        in_specs=(
            P(None, "band", "slab", None, None),
            P("band"),
            P("slab", None, None),
            P("slab", None, None),
        ),
        out_specs=(P(None, "band", "slab", None, None), P("slab", None, None)),
        check_vma=False,
    )
```

time: 252 us -> 131 us (0.52)
  waiting for transfers between devices: 150 us -> 0 us
  Pallas kernels: 0 us -> 119 us
  starting transfers between devices: 36.7 us -> 0 us
  matrix products: 21.4 us -> 0 us
  between operations: 14.3 us -> 0.65 us
  local copies, waits for them, and re-layouts: 21.9 us -> 8.49 us
  other arithmetic: 5.54 us -> 2.47 us
    pallas_call x0 -> x1, Pallas kernels: none -> 119 us  [local(): pl.pallas_call(kernel, out_shape=(jax.ShapeDtypeStruct(orbitals.shape, jn...]
    all_to_all x4 -> x0, waiting for transfers between devices: 98.7 us -> none  [the longest x1 52 us: local(): lax.all_to_all(orbitals, 'slab', split_axis=3, concat_axis=2, tiled=True)]
    psum x1 -> x0, waiting for transfers between devices: 51.7 us -> none  [local(): density = rest_density + lax.psum(partial_sum, 'band')]
    all_to_all x4 -> x0, starting transfers between devices: 36.7 us -> none  [the longest x1 10.2 us: local(): lax.all_to_all(spectrum, 'slab', split_axis=1, concat_axis=0, tiled=True)]
    dot_general x9 -> x0, matrix products: 21.4 us -> none  [product(): return jnp.einsum(spec, a, b, precision=lax.Precision.HIGHEST)]
    all_to_all x4 -> x0, local copies, waits for them, and re-layouts: 7.36 us -> none  [the longest x1 4.69 us: local(): lax.all_to_all(product('poxyz,xk->pokyz', pencil, kinetic), 'slab', split...]
    transpose x2 -> x0, local copies, waits for them, and re-layouts: 6 us -> none  [product(): return jnp.einsum(spec, a, b, precision=lax.Precision.HIGHEST)]
    reduce_sum x1 -> x0, other arithmetic: 2.76 us -> none  [local(): partial_sum = jnp.sum(occupations[:, None, None, None] * squares, axis=0)]
  transfers between devices with their start and end apart: 5 -> 0, of which waited for: 4 -> 0; matrix products, arithmetic and copies ran while one was open for 12% -> 0% of each run, Pallas kernels for 0% -> 0%
where the time goes in v2:
time: 131 us
  Pallas kernels  119 us (91%)
  local copies, waits for them, and re-layouts  8.49 us (6%)
  other arithmetic  2.47 us (2%)
    pallas_call x1, Pallas kernels, local(): pl.pallas_call(kernel, out_shape=(jax.ShapeDtypeStruct(orbitals.shape, jn...  119 us
    unnamed x17, local copies, waits for them, and re-layouts  8.49 us

profile of v2, /device:TPU:1, one launch (start us, length us, event | category | flops | bytes accessed | tf_op | source)
XLA Modules:
  0.0 130.5 jit_solution(12438314502440172692)
XLA Ops:
  0.6 0.0 copy-start
  0.6 2.2 %copy-done = f32[2,16,2,128,128]{4,3,2,1,0:T(8,128)S(1)} copy-done((f32[2,16,2,128,128]{4,3,2,1,0:T(8,128)S(1)}, f32[2,16,2,128,128]{4,3,2,1,0:T(8,128)}, u32[]{:S(2)}) %copy-start) | copy-done | bytes 4194328
  2.8 0.0 copy-start.1
  2.8 0.9 copy-done.1
  3.7 0.0 copy-start.2
  3.7 0.9 copy-done.2
  4.6 0.0 copy-start.3
  4.6 0.7 copy-done.3
  5.3 0.0 copy-start.4
  5.3 0.8 copy-done.4
  6.1 0.0 copy-start.5
  6.1 0.8 copy-done.5
  7.0 0.0 copy-start.6
  7.0 0.8 copy-done.6
  7.7 0.0 copy-start.7
  7.7 0.8 copy-done.7
  8.5 118.9 %shard_map.86 = (f32[2,16,2,128,128]{4,3,2,1,0:T(8,128)S(1)}, f32[2,128,128]{2,1,0:T(8,128)S(1)}) custom-call(bf16[128,128]{1,0:T(8,128)(2,1)S(1)} %copy-done.7, bf16[128,128]{1,0:T(8,128)(2,1)S(1)} %copy-done.6, f32[128,128]{1,0:T(8,128)S(1)} %copy-done.5, f32[128,128]{1,0:T(8,128)S(1)} %copy-done.4, f32[16]{0:T(128)S(1)} %copy-done.3, ...), custom_call_target="tpu_custom_call" | custom-call | flops 10000000000 | bytes 33554432 | tf_op jit(solution)/shard_map/pallas_call | solution.py:308
  127.4 2.5 %broadcast_multiply_fusion = f32[2,16,2,128,128]{4,3,2,1,0:T(8,128)} fusion(f32[2,16,2,128,128]{4,3,2,1,0:T(8,128)S(1)} %get-tuple-element.4), kind=kLoop, calls=%fused_computation | loop fusion | flops 1048576 | bytes 8388608 | tf_op jit(solution)/shard_map/mul | solution.py:327
  129.8 0.7 copy.10
Async XLA Ops:
  0.6 2.2 %copy-start = (f32[2,16,2,128,128]{4,3,2,1,0:T(8,128)S(1)}, f32[2,16,2,128,128]{4,3,2,1,0:T(8,128)}, u32[]{:S(2)}) copy-start(f32[2,16,2,128,128]{4,3,2,1,0:T(8,128)} %psi_hbm.1) | copy-start | bytes 12582916
  2.8 0.9 copy-start.1
  3.7 0.9 copy-start.2
  4.6 0.7 copy-start.3
  5.3 0.8 copy-start.4
  6.1 0.8 copy-start.5
  7.0 0.8 copy-start.6
  7.7 0.8 copy-start.7
